TPU v7x, 32 devices: a whole 2x2x4 slice. The times are simulated.
32 devices in a mesh: tensor: 4 (over z), expert: 8 (over y, x, core).
Axes of the slice: x: 2, y: 2, z: 4, core: 2. Of those that a mesh axis runs over, the one named last changes fastest.
Arguments:
- tokens: bfloat16 [1024, 7168], P('expert', 'tensor'), may hold values from -6 to 6
- route_ids: int32 [1024, 2], P('expert'), may hold values from 0 to 7, all different within a row; in each aligned block of 128 rows (0 to 127, 128 to 255, ...) at most 64 rows name the same one
- route_weights: float32 [1024, 2], P('expert'), may hold values from 0.1 to 1
- cotangent: bfloat16 [1024, 7168], P('expert', 'tensor'), may hold values from -6 to 6
- w_gate: bfloat16 [8, 7168, 1024], P('expert', None, 'tensor'), may hold values from -0.0625 to 0.0625
- w_up: bfloat16 [8, 7168, 1024], P('expert', None, 'tensor'), may hold values from -0.0625 to 0.0625
- w_down: bfloat16 [8, 1024, 7168], P('expert', 'tensor'), may hold values from -0.1875 to 0.1875
Outputs:
- mixed: bfloat16 [1024, 7168], P('expert', 'tensor')
- grad_tokens: bfloat16 [1024, 7168], P('expert', 'tensor')
- grad_route: float32 [1024, 2], P('expert')
- grad_gate: bfloat16 [8, 7168, 1024], P('expert', None, 'tensor')
- grad_up: bfloat16 [8, 7168, 1024], P('expert', None, 'tensor')
- grad_down: bfloat16 [8, 1024, 7168], P('expert', 'tensor')
Inputs may be any that keep to these rules, and one draw needn't show every extreme that they name: `route_ids`: each row names 2 different experts. In each aligned block of 128 rows (the rows of one device) no expert is named by more than 64 rows, and in some block one expert is named by exactly 64 rows.
All inputs are finite; a program needn't handle non-finite values.
Results may differ from a plain program's by a relative error of at most 0.015.
Values may be sent and summed in bfloat16 or wider, within the bound.
No kernel may reach another device: no remote copies, remote signals or barrier semaphores. Data moves between devices by JAX's collectives and lax.ppermute only.
A program may use at most 128 MiB of HBM per device.

v0:
```python
import jax
import jax.numpy as jnp
from jax import lax
from jax.sharding import PartitionSpec as P

TOPK = 2


ROW_PAIRS = (((1,), (1,)), ((), ()))
COLUMN_PAIRS = (((0,), (0,)), ((), ()))


def slot_tables(route_ids, experts, capacity):
    pair_count = route_ids.shape[0] * route_ids.shape[1]
    flat_ids = route_ids.reshape(pair_count)
    labels = jnp.arange(experts, dtype=jnp.int32)
    onehot = (flat_ids[:, None] == labels[None, :]).astype(jnp.int32)
    before = jnp.cumsum(onehot, axis=0) - onehot
    slot_index = jnp.sum(before * onehot, axis=1)
    target = flat_ids * capacity + slot_index
    source = (
        jnp.full((experts * capacity,), pair_count, jnp.int32)
        .at[target]
        .set(jnp.arange(pair_count, dtype=jnp.int32))
    )
    return (target, source)


def fill_slots(token_part, cot_part, weight_flat, source):
    row_of = source // TOPK
    zero_row = jnp.zeros((1, token_part.shape[1]), jnp.bfloat16)
    padded_tokens = jnp.concatenate([token_part, zero_row], axis=0)
    padded_cot = jnp.concatenate([cot_part, zero_row], axis=0)
    padded_weight = jnp.concatenate([weight_flat, jnp.zeros((1,), jnp.float32)], axis=0)
    token_slots = padded_tokens[row_of]
    cot_slots = (padded_weight[source][:, None] * padded_cot[row_of].astype(jnp.float32)).astype(
        jnp.bfloat16
    )
    return (token_slots, cot_slots)


def local(tokens, route_ids, route_weights, cotangent, w_gate, w_up, w_down):
    experts = lax.axis_size("expert")
    tok_rows, slice_width = tokens.shape
    capacity = 4 * tok_rows // experts
    gate_matrix = w_gate[0]
    up_matrix = w_up[0]
    down_weight = w_down[0]
    target, source = slot_tables(route_ids, experts, capacity)
    weight_flat = route_weights.reshape(tok_rows * TOPK)
    full_tokens, full_cot = (
        lax.all_gather(tokens, "tensor", axis=1, tiled=True),
        lax.all_gather(cotangent, "tensor", axis=1, tiled=True),
    )
    model_width = full_tokens.shape[1]
    token_slots, cot_slots = fill_slots(full_tokens, full_cot, weight_flat, source)
    routed, routed_cot = (
        lax.all_to_all(
            token_slots.reshape(experts, capacity, model_width),
            "expert",
            split_axis=0,
            concat_axis=0,
            tiled=True,
        ),
        lax.all_to_all(
            cot_slots.reshape(experts, capacity, model_width),
            "expert",
            split_axis=0,
            concat_axis=0,
            tiled=True,
        ),
    )
    routed = routed.reshape(experts * capacity, model_width)
    routed_cot = routed_cot.reshape(experts * capacity, model_width)
    gate_proj = jnp.dot(routed, gate_matrix, preferred_element_type=jnp.float32)
    up_proj = jnp.dot(routed, up_matrix, preferred_element_type=jnp.float32)
    hidden_state = (jax.nn.silu(gate_proj) * up_proj).astype(jnp.bfloat16)
    down_part = jnp.dot(hidden_state, down_weight, preferred_element_type=jnp.float32)
    expert_sum = lax.psum_scatter(
        down_part.astype(jnp.bfloat16), "tensor", scatter_dimension=1, tiled=True
    )
    expert_output = expert_sum.reshape(experts, capacity, slice_width)
    returned = lax.all_to_all(
        expert_output, "expert", split_axis=0, concat_axis=0, tiled=True
    ).reshape(experts * capacity, slice_width)
    chosen = returned[target].astype(jnp.float32).reshape(tok_rows, TOPK, slice_width)
    mixed = jnp.sum(route_weights[:, :, None] * chosen, axis=1).astype(jnp.bfloat16)
    route_part = jnp.sum(cotangent.astype(jnp.float32)[:, None, :] * chosen, axis=2)
    grad_route = lax.psum(route_part, "tensor")
    d_hidden = lax.dot_general(
        routed_cot, down_weight, ROW_PAIRS, preferred_element_type=jnp.float32
    )
    grad_down = lax.dot_general(
        hidden_state, routed_cot, COLUMN_PAIRS, preferred_element_type=jnp.float32
    ).astype(jnp.bfloat16)
    sigmoid_gate = jax.nn.sigmoid(gate_proj)
    gate_gradient = (
        d_hidden * up_proj * sigmoid_gate * (1.0 + gate_proj * (1.0 - sigmoid_gate))
    ).astype(jnp.bfloat16)
    up_gradient = (d_hidden * jax.nn.silu(gate_proj)).astype(jnp.bfloat16)
    grad_gate = lax.dot_general(
        routed, gate_gradient, COLUMN_PAIRS, preferred_element_type=jnp.float32
    ).astype(jnp.bfloat16)
    grad_up = lax.dot_general(
        routed, up_gradient, COLUMN_PAIRS, preferred_element_type=jnp.float32
    ).astype(jnp.bfloat16)
    back_part = lax.dot_general(
        gate_gradient, gate_matrix, ROW_PAIRS, preferred_element_type=jnp.float32
    )
    back_part = back_part + lax.dot_general(
        up_gradient, up_matrix, ROW_PAIRS, preferred_element_type=jnp.float32
    )
    input_sum = lax.psum_scatter(
        back_part.astype(jnp.bfloat16), "tensor", scatter_dimension=1, tiled=True
    )
    input_rows = input_sum.reshape(experts, capacity, slice_width)
    returned_grads = lax.all_to_all(
        input_rows, "expert", split_axis=0, concat_axis=0, tiled=True
    ).reshape(experts * capacity, slice_width)
    chosen_grads = returned_grads[target].astype(jnp.float32).reshape(tok_rows, TOPK, slice_width)
    grad_tokens = jnp.sum(route_weights[:, :, None] * chosen_grads, axis=1).astype(jnp.bfloat16)
    return (mixed, grad_tokens, grad_route, grad_gate[None], grad_up[None], grad_down[None])


def solution(mesh):
    placed = (
        P("expert", "tensor"),
        P("expert", None),
        P("expert", None),
        P("expert", "tensor"),
        P("expert", None, "tensor"),
        P("expert", None, "tensor"),
        P("expert", "tensor", None),
    )
    return jax.shard_map(
        local,
        mesh=mesh,
        in_specs=placed,
        out_specs=(
            P("expert", "tensor"),
            P("expert", "tensor"),
            P("expert", None),
            P("expert", None, "tensor"),
            P("expert", None, "tensor"),
            P("expert", "tensor", None),
        ),
        check_vma=False,
    )
```

profile of v0, /device:TPU:0, one launch (start us, length us, event | category | flops | bytes accessed | tf_op | source)
XLA Modules:
  0.0 574.8 jit_solution(14941649647857280644)
XLA Ops:
  7.2 0.0 all-gather.3.cloned.1.call-start
  7.2 0.7 all-gather.3.cloned.1.call-update
  7.9 0.8 copy.21
  8.7 0.1 eq.29
  8.8 0.1 eq.25
  9.0 0.7 broadcast_multiply_fusion
  9.7 0.1 copy.20
  9.8 0.1 mul.82
  9.9 0.6 reduce-window.6
  10.5 0.2 slice_reduce_fusion
  10.8 0.1 fusion.16
  10.9 1.4 scatter_custom_fusion
  12.3 41.4 %all-gather.3.cloned.1.call-done = bf16[128,7168]{1,0:T(8,128)(2,1)} async-done(((bf16[128,1792]{1,0:T(8,128)(2,1)}), bf16[128,7168]{1,0:T(8,128)(2,1)}) %all-gather.3.cloned.1.call-update) | async-done | bytes 1835024 | tf_op jit(solution)/shard_map/all_gather | solution.py:52
  53.7 1.7 concatenate.9
  55.4 7.1 %gather_fusion = bf16[512,7168]{1,0:T(8,128)(2,1)} fusion(bf16[129,7168]{1,0:T(8,128)(2,1)S(1)} %concatenate.9, s32[1024]{0:T(1024)S(1)} %pad_clamp_fusion.2), kind=kCustom, calls=%fused_computation | custom fusion | bytes 14682112 | tf_op jit(solution)/shard_map/gather | solution.py:35
  62.4 5.0 all-to-all-start
  67.4 0.0 all-gather.5.cloned.1.call-start
  67.5 0.7 all-gather.5.cloned.1.call-update
  68.2 0.0 copy-done.4
  68.2 0.1 copy.19
  68.3 0.1 reshape.117
  68.5 3.5 gather_fusion.2
  72.0 0.1 mul.87
  72.0 38.7 %all-gather.5.cloned.1.call-done = bf16[128,7168]{1,0:T(8,128)(2,1)} async-done(((bf16[128,1792]{1,0:T(8,128)(2,1)}), bf16[128,7168]{1,0:T(8,128)(2,1)}) %all-gather.5.cloned.1.call-update) | async-done | bytes 1835024 | tf_op jit(solution)/shard_map/all_gather | solution.py:53
  110.7 1.7 concatenate.11
  112.4 7.0 %gather_fusion.3 = bf16[512,7168]{1,0:T(8,128)(2,1)} fusion(bf16[129,7168]{1,0:T(8,128)(2,1)S(1)} %concatenate.11, s32[1024]{0:T(1024)S(1)} %pad_clamp_fusion.2), kind=kCustom, calls=%fused_computation.3 | custom fusion | bytes 14682112 | tf_op jit(solution)/shard_map/gather | solution.py:36
  119.4 8.6 %fusion = bf16[8,64,7168]{2,1,0:T(8,128)(2,1)} fusion(bf16[8,64,7168]{2,1,0:T(8,128)(2,1)} %bitcast.57, f32[8,64]{1,0:T(8,128)S(1)} %mul.87), kind=kLoop, calls=%fused_computation.7 | loop fusion | flops 11010048 | bytes 14682112 | tf_op jit(solution)/shard_map/convert_element_type | solution.py:36
  128.0 22.3 %all-to-all-done = bf16[8,64,7168]{2,1,0:T(8,128)(2,1)} async-done(((bf16[8,64,7168]{2,1,0:T(8,128)(2,1)}), bf16[8,64,7168]{2,1,0:T(8,128)(2,1)}, u32[]{:S(2)}, u32[]{:S(2)}) %all-to-all-start) | async-done | bytes 7340064 | tf_op jit(solution)/shard_map/all_to_all | solution.py:58
  150.2 4.9 all-to-all-start.2
  155.1 0.2 reduce-scatter.3.cloned.1.call-start
  155.3 0.0 copy-start.2
  155.3 6.3 %fusion.8 = f32[512,256]{1,0:T(8,128)S(1)} fusion(bf16[512,7168]{1,0:T(8,128)(2,1)} %bitcast.5, bf16[1,7168,256]{2,1,0:T(8,128)(2,1)} %param.12), kind=kOutput, calls=%fused_computation.20 | convolution fusion | flops 1879048192 | bytes 11534336 | tf_op jit(solution)/shard_map/dot_general | solution.py:76
  161.7 0.0 copy-done.2
  161.7 5.2 fusion.12
  166.9 71.1 %all-to-all-done.2 = bf16[8,64,7168]{2,1,0:T(8,128)(2,1)} async-done(((bf16[8,64,7168]{2,1,0:T(8,128)(2,1)}), bf16[8,64,7168]{2,1,0:T(8,128)(2,1)}, u32[]{:S(2)}, u32[]{:S(2)}) %all-to-all-start.2) | async-done | bytes 7340064 | tf_op jit(solution)/shard_map/all_to_all | solution.py:65
  237.9 6.5 %multiply_convert_fusion = (bf16[512,256]{1,0:T(8,128)(2,1)S(1)}, bf16[512,256]{1,0:T(8,128)(2,1)S(1)}, bf16[512,256]{1,0:T(8,128)(2,1)S(1)}) fusion(f32[512,256]{1,0:T(8,128)S(1)} %fusion.12, f32[512,256]{1,0:T(8,128)S(1)} %fusion.8, bf16[512,7168]{1,0:T(8,128)(2,1)} %bitcast.12, bf16[1,256,7168]{2,1,0:T(8,128)(2,1)} %param.13), kind=kOutput, calls=%fused_computation.29 | convolution fusion | flops 1881014272 | bytes 12845056 | tf_op jit(solution)/shard_map/dot_general | solution.py:90
  244.4 0.0 copy-done.1
  244.4 5.1 convolution_convert_fusion
  249.5 0.0 reduce-scatter.3.cloned.1.call-update
  249.5 0.0 reduce-scatter.5.cloned.1.call-start
  249.6 0.0 copy-start
  249.6 9.5 %fusion.10 = f32[512,7168]{1,0:T(8,128)} fusion(bf16[512,256]{1,0:T(8,128)(2,1)S(1)} %get-tuple-element.16, bf16[1,7168,256]{2,1,0:T(8,128)(2,1)} %param.11), kind=kOutput, calls=%fused_computation.22 | convolution fusion | flops 1879048192 | bytes 18612224 | tf_op jit(solution)/shard_map/dot_general | solution.py:107
  259.1 0.0 copy-done
  259.1 10.4 %add_convert_fusion = bf16[512,7168]{1,0:T(8,128)(2,1)} fusion(f32[512,7168]{1,0:T(8,128)} %fusion.10, bf16[512,256]{1,0:T(8,128)(2,1)S(1)} %get-tuple-element.15, bf16[1,7168,256]{2,1,0:T(8,128)(2,1)S(1)} %copy-done), kind=kOutput, calls=%fused_computation.8 | convolution fusion | flops 1886388224 | bytes 25952256 | tf_op jit(solution)/shard_map/dot_general | solution.py:110
  269.5 0.0 reduce-scatter.5.cloned.1.call-update
  269.5 0.0 copy-start.3
  269.5 105.1 %reduce-scatter.3.cloned.1.call-done = bf16[512,1792]{1,0:T(8,128)(2,1)} async-done(((bf16[512,7168]{1,0:T(8,128)(2,1)}), bf16[512,1792]{1,0:T(8,128)(2,1)}) %reduce-scatter.3.cloned.1.call-update) | async-done | bytes 1835024 | tf_op jit(solution)/shard_map/reduce_scatter | solution.py:79
  374.7 3.7 all-to-all-start.1
  378.3 0.0 copy-done.3
  378.3 1.1 convert_element_type.85
  379.4 125.7 %reduce-scatter.5.cloned.1.call-done = bf16[512,1792]{1,0:T(8,128)(2,1)} async-done(((bf16[512,7168]{1,0:T(8,128)(2,1)}), bf16[512,1792]{1,0:T(8,128)(2,1)}) %reduce-scatter.5.cloned.1.call-update) | async-done | bytes 1835024 | tf_op jit(solution)/shard_map/reduce_scatter | solution.py:113
  505.1 0.0 all-to-all-done.1
  505.1 4.5 all-to-all-start.3
  509.6 7.0 %fusion.3 = bf16[1,256,7168]{2,1,0:T(8,128)(2,1)} fusion(bf16[512,256]{1,0:T(8,128)(2,1)S(1)} %get-tuple-element.17, bf16[512,7168]{1,0:T(8,128)(2,1)} %bitcast.12), kind=kOutput, calls=%fused_computation.15 | convolution fusion | flops 1880883200 | bytes 11272192 | tf_op jit(solution)/shard_map/dot_general | solution.py:93
  516.7 7.1 %fusion.2 = bf16[1,7168,256]{2,1,0:T(8,128)(2,1)} fusion(bf16[512,7168]{1,0:T(8,128)(2,1)} %bitcast.5, bf16[512,256]{1,0:T(8,128)(2,1)S(1)} %get-tuple-element.15), kind=kOutput, calls=%fused_computation.14 | convolution fusion | flops 1880883200 | bytes 11272192 | tf_op jit(solution)/shard_map/dot_general | solution.py:104
  523.7 7.0 %fusion.1 = bf16[1,7168,256]{2,1,0:T(8,128)(2,1)} fusion(bf16[512,7168]{1,0:T(8,128)(2,1)} %bitcast.5, bf16[512,256]{1,0:T(8,128)(2,1)S(1)} %get-tuple-element.16), kind=kOutput, calls=%fused_computation.13 | convolution fusion | flops 1880883200 | bytes 11272192 | tf_op jit(solution)/shard_map/dot_general | solution.py:101
  530.8 1.3 gather_fusion.1
  532.1 0.9 reshape.121
  533.0 0.5 all-to-all-done.3
  533.5 3.9 gather_fusion.4
  537.4 2.1 reshape.123
  539.5 8.7 %multiply_reduce_fusion = (f32[128,2]{1,0:T(8,128)S(1)}, bf16[128,1792]{1,0:T(8,128)(2,1)}, bf16[128,1792]{1,0:T(8,128)(2,1)}) fusion(f32[128,2,1792]{2,1,0:T(2,128)S(1)} %reshape.121, f32[128,1792]{1,0:T(8,128)} %convert_element_type.85, f32[128,2]{1,0:T(8,128)S(1)} %copy.19, f32[128,2,1792]{2,1,0:T(2,128)} %reshape.123), kind=kLoop, calls=%fused_computation.26 | loop fusion | flops 2293504 | bytes 5507072 | tf_op jit(solution)/shard_map/reduce_sum | solution.py:88
  548.2 18.9 %psum.7 = f32[128,2]{1,0:T(8,128)S(1)} all-reduce(f32[128,2]{1,0:T(8,128)S(1)} %get-tuple-element.12), channel_id=1, replica_groups=mesh['tensor'=4,'expert'=8] {'tensor'}, use_global_device_ids=true, to_apply=%region_9.10 | all-reduce | flops 256 | bytes 2048 | tf_op jit(solution)/shard_map/psum | solution.py:89
  567.1 0.6 copy.24
  (12 shorter events, 0.1 us)
Async XLA Ops:
  7.2 46.5 %all-gather.3.cloned.1.call-start = ((), (), s32[]{:S(2)}) async-start(), calls=%async_computation.6 | async-start | bytes 2293760 | tf_op jit(solution)/shard_map/all_gather | solution.py:52
  62.4 5.7 copy-start.4
  62.4 87.8 %all-to-all-start = ((bf16[8,64,7168]{2,1,0:T(8,128)(2,1)}), bf16[8,64,7168]{2,1,0:T(8,128)(2,1)}, u32[]{:S(2)}, u32[]{:S(2)}) async-start(bf16[8,64,7168]{2,1,0:T(8,128)(2,1)} %bitcast.56), calls=%async_computation | async-start | bytes 14680064 | tf_op jit(solution)/shard_map/all_to_all | solution.py:58
  67.4 43.3 %all-gather.5.cloned.1.call-start = ((), (), s32[]{:S(2)}) async-start(), calls=%async_computation.8 | async-start | bytes 2293760 | tf_op jit(solution)/shard_map/all_gather | solution.py:53
  150.2 87.7 %all-to-all-start.2 = ((bf16[8,64,7168]{2,1,0:T(8,128)(2,1)}), bf16[8,64,7168]{2,1,0:T(8,128)(2,1)}, u32[]{:S(2)}, u32[]{:S(2)}) async-start(bf16[8,64,7168]{2,1,0:T(8,128)(2,1)} %fusion), calls=%async_computation.3 | async-start | bytes 14680064 | tf_op jit(solution)/shard_map/all_to_all | solution.py:65
  155.1 219.5 %reduce-scatter.3.cloned.1.call-start = ((), (), s32[]{:S(2)}) async-start(), calls=%async_computation.7 | async-start | bytes 9175040 | tf_op jit(solution)/shard_map/reduce_scatter | solution.py:79
  155.3 6.4 %copy-start.2 = (bf16[1,7168,256]{2,1,0:T(8,128)(2,1)S(1)}, bf16[1,7168,256]{2,1,0:T(8,128)(2,1)}, u32[]{:S(2)}) copy-start(bf16[1,7168,256]{2,1,0:T(8,128)(2,1)} %param.11) | copy-start | bytes 11010052
  237.9 6.5 %copy-start.1 = (bf16[1,256,7168]{2,1,0:T(8,128)(2,1)S(1)}, bf16[1,256,7168]{2,1,0:T(8,128)(2,1)}, u32[]{:S(2)}) copy-start(bf16[1,256,7168]{2,1,0:T(8,128)(2,1)} %param.13) | copy-start | bytes 11010052
  249.5 255.5 %reduce-scatter.5.cloned.1.call-start = ((), (), s32[]{:S(2)}) async-start(), calls=%async_computation.9 | async-start | bytes 9175040 | tf_op jit(solution)/shard_map/reduce_scatter | solution.py:113
  249.6 9.5 %copy-start = (bf16[1,7168,256]{2,1,0:T(8,128)(2,1)S(1)}, bf16[1,7168,256]{2,1,0:T(8,128)(2,1)}, u32[]{:S(2)}) copy-start(bf16[1,7168,256]{2,1,0:T(8,128)(2,1)} %param.12) | copy-start | bytes 11010052
  269.5 108.8 %copy-start.3 = (bf16[128,1792]{1,0:T(8,128)(2,1)S(1)}, bf16[128,1792]{1,0:T(8,128)(2,1)}, u32[]{:S(2)}) copy-start(bf16[128,1792]{1,0:T(8,128)(2,1)} %param.10) | copy-start | bytes 1376260
  374.7 130.4 %all-to-all-start.1 = ((bf16[8,64,1792]{2,1,0:T(8,128)(2,1)}), bf16[8,64,1792]{2,1,0:T(8,128)(2,1)S(1)}, u32[]{:S(2)}, u32[]{:S(2)}) async-start(bf16[8,64,1792]{2,1,0:T(8,128)(2,1)} %bitcast.59), calls=%async_computation.2 | async-start | bytes 3670016 | tf_op jit(solution)/shard_map/all_to_all | solution.py:83
  505.1 28.4 %all-to-all-start.3 = ((bf16[8,64,1792]{2,1,0:T(8,128)(2,1)}), bf16[8,64,1792]{2,1,0:T(8,128)(2,1)}, u32[]{:S(2)}, u32[]{:S(2)}) async-start(bf16[8,64,1792]{2,1,0:T(8,128)(2,1)} %bitcast.58), calls=%async_computation.5 | async-start | bytes 3670016 | tf_op jit(solution)/shard_map/all_to_all | solution.py:117
Sparse Core Ops, SparseCore 0:
  9.6 44.0 all-gather.2
  69.8 40.8 all-gather.4
  249.7 124.9 reduce-scatter.2
  376.8 128.2 reduce-scatter.4
where the time goes:
time: 582 us; the launch traced here: 575 us
  waiting for transfers between devices  406 us (70%)
  matrix products  64.1 us (11%)
  local copies, waits for them, and re-layouts  33.1 us (6%)
  other arithmetic  19.8 us (3%)
  blocking collectives  18.9 us (3%)
  starting transfers between devices  18.4 us (3%)
  between operations  14.4 us (2%)
    reduce_scatter x1, waiting for transfers between devices, local(): lax.psum_scatter(back_part.astype(jnp.bfloat16), 'tensor', scatter_dimens...  126 us
    reduce_scatter x1, waiting for transfers between devices, local(): lax.psum_scatter(down_part.astype(jnp.bfloat16), 'tensor', scatter_dimens...  105 us
    all_to_all x1, waiting for transfers between devices, local(): lax.all_to_all(cot_slots.reshape(experts, capacity, model_width), 'expert...  71.1 us
    all_gather x1, waiting for transfers between devices, local(): lax.all_gather(tokens, 'tensor', axis=1, tiled=True)  41.4 us
    all_gather x1, waiting for transfers between devices, local(): lax.all_gather(cotangent, 'tensor', axis=1, tiled=True)  38.7 us
    all_to_all x1, waiting for transfers between devices, local(): lax.all_to_all(token_slots.reshape(experts, capacity, model_width), 'expe...  22.3 us
    psum x1, blocking collectives, local(): grad_route = lax.psum(route_part, 'tensor')  18.9 us
  transfers between devices with their start and end apart: 8, of which 7 were waited for; matrix products, arithmetic and copies ran while one was open for 14% of the time, Pallas kernels for 0%

commit v1 on v0

--- a/solution.py
+++ b/solution.py
@@ -39,7 +39,7 @@
     return (token_slots, cot_slots)
 
 
-def local(tokens, route_ids, route_weights, cotangent, w_gate, w_up, w_down):
+def slot_plan(tokens, route_ids, route_weights, cotangent, w_gate, w_up, w_down):
     experts = lax.axis_size("expert")
     tok_rows, slice_width = tokens.shape
     capacity = 4 * tok_rows // experts
@@ -122,6 +122,176 @@
     return (mixed, grad_tokens, grad_route, grad_gate[None], grad_up[None], grad_down[None])
 
 
+def xor_pairs(bit):
+    return [(i, i ^ bit) for i in range(lax.axis_size("expert"))]
+
+
+def over_core(value):
+    return lax.ppermute(value, "expert", xor_pairs(1))
+
+
+def over_x(value):
+    return lax.ppermute(value, "expert", xor_pairs(2))
+
+
+def over_y(value):
+    return lax.ppermute(value, "expert", xor_pairs(4))
+
+
+def over_z(value):
+    count = lax.axis_size("tensor")
+    return lax.ppermute(value, "tensor", [(i, (i + 1) % count) for i in range(count)])
+
+
+def gather_rows(part, count):
+    pieces = []
+    own = part
+    for step in range(count):
+        side, front = over_x(own), over_y(own)
+        far = over_y(side) if step % 2 == 0 else over_x(front)
+        pieces.append(jnp.concatenate([own, side, front, far], axis=0))
+        if step < count - 1:
+            own = over_z(own)
+    return pieces
+
+
+def scatter_rows(product, rows, count, place):
+    def rounded(blocks, part):
+        return product(blocks, part).astype(jnp.bfloat16)
+
+    total = None
+    for step in range(count):
+        part = lax.rem(place + 2 * count - 1 - step, count)
+        if step % 2 == 0:
+            came = over_x(rounded((1, 3), part))
+            kept = (product((0, 2), part) + came.astype(jnp.float32))
+            last = over_y(kept[rows:].astype(jnp.bfloat16))
+        else:
+            came = over_y(rounded((2, 3), part))
+            kept = (product((0, 1), part) + came.astype(jnp.float32))
+            last = over_x(kept[rows:].astype(jnp.bfloat16))
+        here = kept[:rows] + last.astype(jnp.float32)
+        if total is not None:
+            here = here + total.astype(jnp.float32)
+        here = here.astype(jnp.bfloat16)
+        total = over_z(here) if step < count - 1 else here
+    return total
+
+
+def dot(a, b, dims=(((1,), (0,)), ((), ()))):
+    return lax.dot_general(a, b, dims, preferred_element_type=jnp.float32)
+
+
+def chip_plan(tokens, route_ids, route_weights, cotangent, w_gate, w_up, w_down):
+    count = lax.axis_size("tensor")
+    experts = lax.axis_size("expert")
+    place, me = lax.axis_index("tensor"), lax.axis_index("expert")
+    rows, width = tokens.shape
+    units = w_gate.shape[2]
+
+    wide = jnp.concatenate([w_gate[0], w_up[0]], axis=1)
+    wide = jnp.concatenate([wide, over_core(wide)], axis=1)
+    tall = jnp.concatenate([w_down[0], over_core(w_down[0])], axis=0)
+
+    labels = jnp.arange(experts, dtype=jnp.int32)
+    named = route_ids[:, :, None] == labels[None, None, :]
+    shares = jnp.sum(jnp.where(named, route_weights[:, :, None], 0.0), axis=1)
+    shares_x, shares_y = over_x(shares), over_y(shares)
+    shares = jnp.concatenate([shares, shares_x, shares_y, over_y(shares_x)], axis=0)
+    share = [
+        lax.dynamic_slice_in_dim(shares, me, 1, 1),
+        lax.dynamic_slice_in_dim(shares, me ^ 1, 1, 1),
+    ]
+
+    def part_of(step):
+        return lax.rem(place + count - step, count)
+
+    def wide_part(part):
+        return lax.dynamic_slice_in_dim(wide, part * width, width, 0)
+
+    def tall_part(part):
+        return lax.dynamic_slice_in_dim(tall, part * width, width, 1)
+
+    token_parts = gather_rows(tokens, count)
+    cot_parts = gather_rows(cotangent, count)
+
+    both = sum(dot(token_parts[k], wide_part(part_of(k))) for k in range(count))
+    d_both = sum(dot(cot_parts[k], tall_part(part_of(k)), ROW_PAIRS) for k in range(count))
+    weighted, to_weights, to_tokens, inner = [], [], [], []
+    for i in range(2):
+        gate = both[:, (2 * i) * units : (2 * i + 1) * units]
+        up = both[:, (2 * i + 1) * units : (2 * i + 2) * units]
+        d_plain = d_both[:, i * units : (i + 1) * units]
+        sigmoid_gate = jax.nn.sigmoid(gate)
+        silu_gate = gate * sigmoid_gate
+        hidden = silu_gate * up
+        weighted.append((share[i] * hidden).astype(jnp.bfloat16))
+        inner.append(jnp.sum(hidden * d_plain, axis=1, keepdims=True))
+        d_hidden = share[i] * d_plain
+        d_gate = d_hidden * up * sigmoid_gate * (1.0 + gate * (1.0 - sigmoid_gate))
+        d_up = d_hidden * silu_gate
+        to_weights += [d_gate.astype(jnp.bfloat16), d_up.astype(jnp.bfloat16)]
+        to_tokens += [(share[i] * d_gate).astype(jnp.bfloat16), (share[i] * d_up).astype(jnp.bfloat16)]
+    weighted = jnp.concatenate(weighted, axis=1)
+    to_tokens = jnp.concatenate(to_tokens, axis=1)
+
+    def blocks_of(matrix, blocks):
+        return jnp.concatenate([matrix[b * rows : (b + 1) * rows] for b in blocks], axis=0)
+
+    mixed = scatter_rows(
+        lambda blocks, part: dot(blocks_of(weighted, blocks), tall_part(part)), rows, count, place
+    )
+    grad_tokens = scatter_rows(
+        lambda blocks, part: dot(blocks_of(to_tokens, blocks), wide_part(part), ROW_PAIRS),
+        rows,
+        count,
+        place,
+    )
+
+    inner = jnp.concatenate(inner, axis=1)
+    turns = [inner]
+    for _ in range(count - 1):
+        turns.append(over_z(turns[-1]))
+    turns = jnp.stack(turns)
+    inner = sum(lax.dynamic_index_in_dim(turns, part_of(k), 0, False) for k in range(count))
+    blocks = [inner[b * rows : (b + 1) * rows] for b in range(4)]
+    inner = [blocks[0], over_x(blocks[1]), over_y(blocks[2]), over_y(over_x(blocks[3]))]
+    grad_route = 0.0
+    for q in range(4):
+        for i in range(2):
+            grad_route += jnp.where(route_ids == me ^ (2 * q) ^ i, inner[q][:, i : i + 1], 0.0)
+
+    own_cols = jnp.concatenate(to_weights[:2], axis=1)
+    other_cols = jnp.concatenate(to_weights[2:], axis=1)
+    grad_wide = [dot(token_parts[k], other_cols, COLUMN_PAIRS).astype(jnp.bfloat16) for k in range(count)]
+    grad_tall = [
+        dot(weighted[:, units:], cot_parts[k], COLUMN_PAIRS).astype(jnp.bfloat16) for k in range(count)
+    ]
+    grad_wide = [over_core(g) for g in grad_wide]
+    grad_tall = [over_core(g) for g in grad_tall]
+    grad_gate = jnp.zeros(w_gate.shape[1:], jnp.bfloat16)
+    grad_up = jnp.zeros(w_up.shape[1:], jnp.bfloat16)
+    grad_down = jnp.zeros(w_down.shape[1:], jnp.bfloat16)
+    for k in range(count):
+        part = part_of(k)
+        both_grads = dot(token_parts[k], own_cols, COLUMN_PAIRS) + grad_wide[k].astype(jnp.float32)
+        both_grads = both_grads.astype(jnp.bfloat16)
+        down = dot(weighted[:, :units], cot_parts[k], COLUMN_PAIRS) + grad_tall[k].astype(jnp.float32)
+        grad_gate = lax.dynamic_update_slice_in_dim(grad_gate, both_grads[:, :units], part * width, 0)
+        grad_up = lax.dynamic_update_slice_in_dim(grad_up, both_grads[:, units:], part * width, 0)
+        grad_down = lax.dynamic_update_slice_in_dim(
+            grad_down, down.astype(jnp.bfloat16), part * width, 1
+        )
+    return (mixed, grad_tokens, grad_route, grad_gate[None], grad_up[None], grad_down[None])
+
+
+def local(tokens, route_ids, route_weights, cotangent, w_gate, w_up, w_down):
+    experts = lax.axis_size("expert")
+    capacity = 4 * tokens.shape[0] // experts
+    plan = chip_plan if 2 * capacity >= tokens.shape[0] and experts == 8 else slot_plan
+    return plan(tokens, route_ids, route_weights, cotangent, w_gate, w_up, w_down)
+
+
 def solution(mesh):
     placed = (
         P("expert", "tensor"),

time: 582 us -> 472 us (0.81); the launches traced: 575 us -> 471 us
  waiting for transfers between devices: 406 us -> 285 us
  starting transfers between devices: 18.4 us -> 58 us
  matrix products: 64.1 us -> 92.2 us
  blocking collectives: 18.9 us -> 0 us
  local copies, waits for them, and re-layouts: 33.1 us -> 14.5 us
  between operations: 14.4 us -> 1.91 us
    ppermute x0 -> x72, waiting for transfers between devices: none -> 285 us  [the longest x15 97.7 us: over_z(): lax.ppermute(value, 'tensor', [(i, (i + 1) % count) for i in range(count)])]
    reduce_scatter x2 -> x0, waiting for transfers between devices: 231 us -> none  [the longest x1 126 us: local(): lax.psum_scatter(back_part.astype(jnp.bfloat16), 'tensor', scatter_dimens...]
    all_to_all x4 -> x0, waiting for transfers between devices: 93.8 us -> none  [the longest x1 71.1 us: local(): lax.all_to_all(cot_slots.reshape(experts, capacity, model_width), 'expert...]
    all_gather x2 -> x0, waiting for transfers between devices: 80 us -> none  [the longest x1 41.4 us: local(): lax.all_gather(tokens, 'tensor', axis=1, tiled=True)]
    ppermute x0 -> x72, starting transfers between devices: none -> 58 us  [the longest x23 26.3 us: over_x(): return lax.ppermute(value, 'expert', xor_pairs(2))]
    dot_general x9 -> x40, matrix products: 64.1 us -> 92.2 us  [dot(): return lax.dot_general(a, b, dims, preferred_element_type=jnp.float32)]
    gather x5 -> x0, local copies, waits for them, and re-layouts: 22.8 us -> none  [the longest x1 7.05 us: fill_slots(): token_slots = padded_tokens[row_of]]
    psum x1 -> x0, blocking collectives: 18.9 us -> none  [local(): grad_route = lax.psum(route_part, 'tensor')]
  transfers between devices with their start and end apart: 8 -> 72, of which waited for: 7 -> 37; matrix products, arithmetic and copies ran while one was open for 14% -> 13% of each run, Pallas kernels for 0% -> 0%
where the time goes in v1:
time: 472 us; the launch traced here: 471 us
  waiting for transfers between devices  285 us (60%)
  matrix products  92.2 us (20%)
  starting transfers between devices  58 us (12%)
  other arithmetic  19.2 us (4%)
  local copies, waits for them, and re-layouts  14.5 us (3%)
    ppermute x15, waiting for transfers between devices, over_z(): lax.ppermute(value, 'tensor', [(i, (i + 1) % count) for i in range(count)])  97.7 us
    ppermute x24, waiting for transfers between devices, over_y(): return lax.ppermute(value, 'expert', xor_pairs(4))  97.5 us
    dot_general x40, matrix products, dot(): return lax.dot_general(a, b, dims, preferred_element_type=jnp.float32)  92.2 us
    ppermute x23, waiting for transfers between devices, over_x(): return lax.ppermute(value, 'expert', xor_pairs(2))  90 us
    ppermute x23, starting transfers between devices, over_x(): return lax.ppermute(value, 'expert', xor_pairs(2))  26.3 us
    ppermute x24, starting transfers between devices, over_y(): return lax.ppermute(value, 'expert', xor_pairs(4))  22.8 us
    unnamed x92, local copies, waits for them, and re-layouts  11.4 us
  transfers between devices with their start and end apart: 72, of which 37 were waited for; matrix products, arithmetic and copies ran while one was open for 13% of the time, Pallas kernels for 0%

profile of v1, /device:TPU:0, one launch (start us, length us, event | category | flops | bytes accessed | tf_op | source)
XLA Modules:
  0.0 471.1 jit_solution(281233161096931460)
XLA Ops:
  0.6 3.1 collective-permute-start.34
  9.5 6.7 %pad_maximum_fusion.1 = bf16[7168,512]{1,0:T(8,128)(2,1)} fusion(bf16[7168,256]{1,0:T(8,128)(2,1)} %bitcast.130, bf16[7168,256]{1,0:T(8,128)(2,1)} %bitcast.132), kind=kLoop, calls=%fused_computation.15 | loop fusion | flops 14680064 | bytes 14680064 | tf_op jit(solution)/shard_map/concatenate | solution.py:192
  23.8 7.1 %collective-permute-done.7 = bf16[128,1792]{1,0:T(8,128)(2,1)S(1)} collective-permute-done((bf16[128,1792]{1,0:T(8,128)(2,1)S(1)}, bf16[128,1792]{1,0:T(8,128)(2,1)S(1)}, u32[]{:S(2)}, u32[]{:S(2)}) %collective-permute-start.7) | collective-permute-done | bytes 458784 | tf_op jit(solution)/shard_map/ppermute | solution.py:143
  35.8 11.1 %collective-permute-done.38 = bf16[128,1792]{1,0:T(8,128)(2,1)S(1)} collective-permute-done((bf16[128,1792]{1,0:T(8,128)(2,1)S(1)}, bf16[128,1792]{1,0:T(8,128)(2,1)S(1)}, u32[]{:S(2)}, u32[]{:S(2)}) %collective-permute-start.38) | collective-permute-done | bytes 458784 | tf_op jit(solution)/shard_map/ppermute | solution.py:143
  47.4 8.4 %collective-permute-done.11 = bf16[128,1792]{1,0:T(8,128)(2,1)S(1)} collective-permute-done((bf16[128,1792]{1,0:T(8,128)(2,1)S(1)}, bf16[128,1792]{1,0:T(8,128)(2,1)S(1)}, u32[]{:S(2)}, u32[]{:S(2)}) %collective-permute-start.11) | collective-permute-done | bytes 458784 | tf_op jit(solution)/shard_map/ppermute | solution.py:143
  59.5 9.7 %collective-permute-done.33 = bf16[128,1792]{1,0:T(8,128)(2,1)S(1)} collective-permute-done((bf16[128,1792]{1,0:T(8,128)(2,1)S(1)}, bf16[128,1792]{1,0:T(8,128)(2,1)S(1)}, u32[]{:S(2)}, u32[]{:S(2)}) %collective-permute-start.33) | collective-permute-done | bytes 458784 | tf_op jit(solution)/shard_map/ppermute | solution.py:138
  69.7 9.3 %collective-permute-done.5 = bf16[128,1792]{1,0:T(8,128)(2,1)S(1)} collective-permute-done((bf16[128,1792]{1,0:T(8,128)(2,1)S(1)}, bf16[128,1792]{1,0:T(8,128)(2,1)S(1)}, u32[]{:S(2)}, u32[]{:S(2)}) %collective-permute-start.5) | collective-permute-done | bytes 458784 | tf_op jit(solution)/shard_map/ppermute | solution.py:138
  80.7 6.3 %collective-permute-done.9 = bf16[128,1792]{1,0:T(8,128)(2,1)S(1)} collective-permute-done((bf16[128,1792]{1,0:T(8,128)(2,1)S(1)}, bf16[128,1792]{1,0:T(8,128)(2,1)S(1)}, u32[]{:S(2)}, u32[]{:S(2)}) %collective-permute-start.9) | collective-permute-done | bytes 458784 | tf_op jit(solution)/shard_map/ppermute | solution.py:138
  87.0 2.6 collective-permute-done.42
  90.2 9.3 %collective-permute-done.15 = bf16[128,1792]{1,0:T(8,128)(2,1)S(1)} collective-permute-done((bf16[128,1792]{1,0:T(8,128)(2,1)S(1)}, bf16[128,1792]{1,0:T(8,128)(2,1)S(1)}, u32[]{:S(2)}, u32[]{:S(2)}) %collective-permute-start.15) | collective-permute-done | bytes 458784 | tf_op jit(solution)/shard_map/ppermute | solution.py:143
  102.2 10.7 %collective-permute-done.37 = bf16[128,1792]{1,0:T(8,128)(2,1)S(1)} collective-permute-done((bf16[128,1792]{1,0:T(8,128)(2,1)S(1)}, bf16[128,1792]{1,0:T(8,128)(2,1)S(1)}, u32[]{:S(2)}, u32[]{:S(2)}) %collective-permute-start.37) | collective-permute-done | bytes 458784 | tf_op jit(solution)/shard_map/ppermute | solution.py:134
  114.4 8.3 %collective-permute-done.12 = bf16[128,1792]{1,0:T(8,128)(2,1)S(1)} collective-permute-done((bf16[128,1792]{1,0:T(8,128)(2,1)S(1)}, bf16[128,1792]{1,0:T(8,128)(2,1)S(1)}, u32[]{:S(2)}, u32[]{:S(2)}) %collective-permute-start.12) | collective-permute-done | bytes 458784 | tf_op jit(solution)/shard_map/ppermute | solution.py:134
  124.9 7.7 %collective-permute-done.10 = bf16[128,1792]{1,0:T(8,128)(2,1)S(1)} collective-permute-done((bf16[128,1792]{1,0:T(8,128)(2,1)S(1)}, bf16[128,1792]{1,0:T(8,128)(2,1)S(1)}, u32[]{:S(2)}, u32[]{:S(2)}) %collective-permute-start.10) | collective-permute-done | bytes 458784 | tf_op jit(solution)/shard_map/ppermute | solution.py:134
  133.1 6.5 %collective-permute-done.43 = bf16[128,1792]{1,0:T(8,128)(2,1)S(1)} collective-permute-done((bf16[128,1792]{1,0:T(8,128)(2,1)S(1)}, bf16[128,1792]{1,0:T(8,128)(2,1)S(1)}, u32[]{:S(2)}, u32[]{:S(2)}) %collective-permute-start.43) | collective-permute-done | bytes 458784 | tf_op jit(solution)/shard_map/ppermute | solution.py:134
  141.8 6.8 %collective-permute-done.16 = bf16[128,1792]{1,0:T(8,128)(2,1)S(1)} collective-permute-done((bf16[128,1792]{1,0:T(8,128)(2,1)S(1)}, bf16[128,1792]{1,0:T(8,128)(2,1)S(1)}, u32[]{:S(2)}, u32[]{:S(2)}) %collective-permute-start.16) | collective-permute-done | bytes 458784 | tf_op jit(solution)/shard_map/ppermute | solution.py:134
  149.1 6.9 %collective-permute-done.17 = bf16[128,1792]{1,0:T(8,128)(2,1)S(1)} collective-permute-done((bf16[128,1792]{1,0:T(8,128)(2,1)S(1)}, bf16[128,1792]{1,0:T(8,128)(2,1)S(1)}, u32[]{:S(2)}, u32[]{:S(2)}) %collective-permute-start.17) | collective-permute-done | bytes 458784 | tf_op jit(solution)/shard_map/ppermute | solution.py:138
  158.1 4.1 collective-permute-done.14
  162.3 4.1 collective-permute-done.45
  166.4 4.9 %collective-permute-done.18 = bf16[128,1792]{1,0:T(8,128)(2,1)S(1)} collective-permute-done((bf16[128,1792]{1,0:T(8,128)(2,1)S(1)}, bf16[128,1792]{1,0:T(8,128)(2,1)S(1)}, u32[]{:S(2)}, u32[]{:S(2)}) %collective-permute-start.18) | collective-permute-done | bytes 458784 | tf_op jit(solution)/shard_map/ppermute | solution.py:134
  179.4 6.4 %pad_maximum_fusion = bf16[7168,1024]{1,0:T(8,128)(2,1)S(1)} fusion(bf16[7168,512]{1,0:T(8,128)(2,1)} %collective-permute-done.6, bf16[7168,256]{1,0:T(8,128)(2,1)S(1)} %bitcast.131, bf16[7168,256]{1,0:T(8,128)(2,1)S(1)} %bitcast.133), kind=kLoop, calls=%fused_computation | loop fusion | flops 44040192 | bytes 29360128 | tf_op jit(solution)/shard_map/concatenate | solution.py:193
  185.8 4.9 %fusion.2 = f32[512,1024]{1,0:T(8,128)} fusion(bf16[512,1792]{1,0:T(8,128)(2,1)} %copy-done.21, bf16[7168,1024]{1,0:T(8,128)(2,1)S(1)} %pad_maximum_fusion, s32[]{:T(128)S(6)} %select_n.102), kind=kOutput, calls=%fused_computation.22 | convolution fusion | flops 1879048192 | bytes 7602180 | tf_op jit(solution)/shard_map/dot_general | solution.py:182
  190.7 3.4 fusion.22
  194.1 3.4 fusion.4
  197.5 4.9 %add_add_fusion = f32[512,1024]{1,0:T(8,128)S(1)} fusion(f32[512,1024]{1,0:T(8,128)} %fusion.2, f32[512,1024]{1,0:T(8,128)} %fusion.22, f32[512,1024]{1,0:T(8,128)} %fusion.4, bf16[512,1792]{1,0:T(8,128)(2,1)S(1)} %copy-done.28, bf16[7168,1024]{1,0:T(8,128)(2,1)S(1)} %pad_maximum_fusion, s32[]{:T(128)S(6)} %select_n.103), kind=kOutput, calls=%fused_computation.84 | convolution fusion | flops 1880621056 | bytes 13893636 | tf_op jit(solution)/shard_map/dot_general | solution.py:182
  205.1 2.1 fusion.36
  208.8 2.4 convolution_convert_fusion.3
  211.2 2.4 convolution_convert_fusion.2
  213.6 2.4 convolution_convert_fusion.1
  216.0 2.4 convolution_convert_fusion
  218.4 14.4 %convolution_convert_fusion.7 = bf16[256,1792]{1,0:T(8,128)(2,1)} fusion(bf16[512,256]{1,0:T(8,128)(2,1)S(1)} %get-tuple-element.24, bf16[512,1792]{1,0:T(8,128)(2,1)S(1)} %copy-done.4), kind=kOutput, calls=%fused_computation.67 | convolution fusion | flops 470220800 | bytes 3014656 | tf_op jit(solution)/shard_map/dot_general | solution.py:182
  234.4 1.7 convolution_convert_fusion.5
  239.4 2.1 fusion.42
  241.6 2.1 fusion.39
  243.7 2.1 fusion.45
  249.2 3.2 collective-permute-done.58
  254.0 3.8 collective-permute-done.59
  260.9 2.0 collective-permute-done.61
  263.5 9.2 %collective-permute-done.62 = f32[128,2]{0,1:T(2,128)S(1)} collective-permute-done((f32[128,2]{0,1:T(2,128)S(1)}, f32[128,2]{0,1:T(2,128)S(1)}, u32[]{:S(2)}, u32[]{:S(2)}) %collective-permute-start.62) | collective-permute-done | bytes 1056 | tf_op jit(solution)/shard_map/ppermute | solution.py:134
  274.7 19.0 %collective-permute-done.63 = f32[128,2]{0,1:T(2,128)S(1)} collective-permute-done((f32[128,2]{0,1:T(2,128)S(1)}, f32[128,2]{0,1:T(2,128)S(1)}, u32[]{:S(2)}, u32[]{:S(2)}) %collective-permute-start.63) | collective-permute-done | bytes 1056 | tf_op jit(solution)/shard_map/ppermute | solution.py:138
  297.8 18.0 %collective-permute-done.46 = bf16[256,1792]{1,0:T(8,128)(2,1)S(1)} collective-permute-done((bf16[256,1792]{1,0:T(8,128)(2,1)}, bf16[256,1792]{1,0:T(8,128)(2,1)S(1)}, u32[]{:S(2)}, u32[]{:S(2)}) %collective-permute-start.46) | collective-permute-done | bytes 917536 | tf_op jit(solution)/shard_map/ppermute | solution.py:138
  316.7 2.3 fusion.24
  319.1 6.5 %collective-permute-done.50 = bf16[256,1792]{1,0:T(8,128)(2,1)S(1)} collective-permute-done((bf16[256,1792]{1,0:T(8,128)(2,1)}, bf16[256,1792]{1,0:T(8,128)(2,1)S(1)}, u32[]{:S(2)}, u32[]{:S(2)}) %collective-permute-start.50) | collective-permute-done | bytes 917536 | tf_op jit(solution)/shard_map/ppermute | solution.py:138
  325.6 2.4 fusion.30
  328.9 1.9 fusion.59
  332.4 1.8 fusion.57
  334.4 1.8 fusion.55
  336.8 1.8 convolution_add_fusion.5
  338.7 1.8 convolution_add_fusion.6
  340.6 10.9 %collective-permute-done.48 = bf16[256,1792]{1,0:T(8,128)(2,1)} collective-permute-done((bf16[256,1792]{1,0:T(8,128)(2,1)}, bf16[256,1792]{1,0:T(8,128)(2,1)}, u32[]{:S(2)}, u32[]{:S(2)}) %collective-permute-start.48) | collective-permute-done | bytes 917536 | tf_op jit(solution)/shard_map/ppermute | solution.py:134
  351.5 2.4 fusion.27
  353.9 16.9 %collective-permute-done.52 = bf16[256,1792]{1,0:T(8,128)(2,1)} collective-permute-done((bf16[256,1792]{1,0:T(8,128)(2,1)}, bf16[256,1792]{1,0:T(8,128)(2,1)}, u32[]{:S(2)}, u32[]{:S(2)}) %collective-permute-start.52) | collective-permute-done | bytes 917536 | tf_op jit(solution)/shard_map/ppermute | solution.py:134
  372.3 2.4 fusion.33
  377.5 5.4 %collective-permute-done.27 = bf16[128,1792]{1,0:T(8,128)(2,1)S(1)} collective-permute-done((bf16[128,1792]{1,0:T(8,128)(2,1)S(1)}, bf16[128,1792]{1,0:T(8,128)(2,1)S(1)}, u32[]{:S(2)}, u32[]{:S(2)}) %collective-permute-start.27) | collective-permute-done | bytes 458784 | tf_op jit(solution)/shard_map/ppermute | solution.py:138
  384.5 9.6 %collective-permute-done.53 = bf16[128,1792]{1,0:T(8,128)(2,1)S(1)} collective-permute-done((bf16[128,1792]{1,0:T(8,128)(2,1)S(1)}, bf16[128,1792]{1,0:T(8,128)(2,1)S(1)}, u32[]{:S(2)}, u32[]{:S(2)}) %collective-permute-start.53) | collective-permute-done | bytes 458784 | tf_op jit(solution)/shard_map/ppermute | solution.py:138
  396.4 3.0 add_convert_fusion.3
  401.0 2.7 add_convert_fusion.2
  405.4 2.6 add_convert_fusion.1
  412.1 8.1 %collective-permute-done.28 = bf16[128,1792]{1,0:T(8,128)(2,1)S(1)} collective-permute-done((bf16[128,1792]{1,0:T(8,128)(2,1)S(1)}, bf16[128,1792]{1,0:T(8,128)(2,1)S(1)}, u32[]{:S(2)}, u32[]{:S(2)}) %collective-permute-start.28) | collective-permute-done | bytes 458784 | tf_op jit(solution)/shard_map/ppermute | solution.py:143
  420.4 4.2 collective-permute-done.51
  425.0 5.9 %collective-permute-done.54 = bf16[128,1792]{1,0:T(8,128)(2,1)S(1)} collective-permute-done((bf16[128,1792]{1,0:T(8,128)(2,1)S(1)}, bf16[128,1792]{1,0:T(8,128)(2,1)S(1)}, u32[]{:S(2)}, u32[]{:S(2)}) %collective-permute-start.54) | collective-permute-done | bytes 458784 | tf_op jit(solution)/shard_map/ppermute | solution.py:143
  431.4 14.7 %collective-permute-done.29 = bf16[128,1792]{1,0:T(8,128)(2,1)S(1)} collective-permute-done((bf16[128,1792]{1,0:T(8,128)(2,1)S(1)}, bf16[128,1792]{1,0:T(8,128)(2,1)S(1)}, u32[]{:S(2)}, u32[]{:S(2)}) %collective-permute-start.29) | collective-permute-done | bytes 458784 | tf_op jit(solution)/shard_map/ppermute | solution.py:143
  446.4 9.6 %collective-permute-done.55 = bf16[128,1792]{1,0:T(8,128)(2,1)S(1)} collective-permute-done((bf16[128,1792]{1,0:T(8,128)(2,1)S(1)}, bf16[128,1792]{1,0:T(8,128)(2,1)S(1)}, u32[]{:S(2)}, u32[]{:S(2)}) %collective-permute-start.55) | collective-permute-done | bytes 458784 | tf_op jit(solution)/shard_map/ppermute | solution.py:143
  456.2 8.8 %collective-permute-done.30 = bf16[128,1792]{1,0:T(8,128)(2,1)S(1)} collective-permute-done((bf16[128,1792]{1,0:T(8,128)(2,1)S(1)}, bf16[128,1792]{1,0:T(8,128)(2,1)S(1)}, u32[]{:S(2)}, u32[]{:S(2)}) %collective-permute-start.30) | collective-permute-done | bytes 458784 | tf_op jit(solution)/shard_map/ppermute | solution.py:143
  465.9 4.0 collective-permute-done.56
  (266 shorter events, 91.8 us)
Async XLA Ops:
  0.6 21.5 %collective-permute-start.34 = (bf16[128,1792]{1,0:T(8,128)(2,1)}, bf16[128,1792]{1,0:T(8,128)(2,1)S(1)}, u32[]{:S(2)}, u32[]{:S(2)}) collective-permute-start(bf16[128,1792]{1,0:T(8,128)(2,1)} %param.10), channel_id=1, source_target_pairs={{0,8},{8,16},{16,24},{24,0},{1,9},{9,17},{17,25},{25,1},{2,10},{10... | collective-permute-start | bytes 1376264 | tf_op jit(solution)/shard_map/ppermute | solution.py:143
  3.7 27.3 %collective-permute-start.31 = (bf16[128,1792]{1,0:T(8,128)(2,1)}, bf16[128,1792]{1,0:T(8,128)(2,1)S(1)}, u32[]{:S(2)}, u32[]{:S(2)}) collective-permute-start(bf16[128,1792]{1,0:T(8,128)(2,1)} %param.10), channel_id=1, source_target_pairs={{0,2},{1,3},{2,0},{3,1},{4,6},{5,7},{6,4},{7,5},{8,10},{9,11},{10,... | collective-permute-start | bytes 1376264 | tf_op jit(solution)/shard_map/ppermute | solution.py:134
  5.2 26.4 %collective-permute-start.32 = (bf16[128,1792]{1,0:T(8,128)(2,1)}, bf16[128,1792]{1,0:T(8,128)(2,1)}, u32[]{:S(2)}, u32[]{:S(2)}) collective-permute-start(bf16[128,1792]{1,0:T(8,128)(2,1)} %param.10), channel_id=1, source_target_pairs={{0,4},{1,5},{2,6},{3,7},{4,0},{5,1},{6,2},{7,3},{8,12},{9,13},{10,... | collective-permute-start | bytes 1376264 | tf_op jit(solution)/shard_map/ppermute | solution.py:138
  8.0 10.6 %collective-permute-start.1 = (f32[128,8]{0,1:T(8,128)S(1)}, f32[128,8]{0,1:T(8,128)S(1)}, u32[]{:S(2)}, u32[]{:S(2)}) collective-permute-start(f32[128,8]{0,1:T(8,128)S(1)} %select_reduce_fusion), channel_id=1, source_target_pairs={{0,4},{1,5},{2,6},{3,7},{4,0},{5,1},{6,2},{7,3},{8,12},{9,13},{10,... | collective-permute-start | bytes 12296 | tf_op jit(solution)/shard_map/ppermute | solution.py:138
  18.6 12.4 %collective-permute-start.7 = (bf16[128,1792]{1,0:T(8,128)(2,1)S(1)}, bf16[128,1792]{1,0:T(8,128)(2,1)S(1)}, u32[]{:S(2)}, u32[]{:S(2)}) collective-permute-start(bf16[128,1792]{1,0:T(8,128)(2,1)S(1)} %copy-done.13), channel_id=1, source_target_pairs={{0,8},{8,16},{16,24},{24,0},{1,9},{9,17},{17,25},{25,1},{2,10},{10... | collective-permute-start | bytes 1376264 | tf_op jit(solution)/shard_map/ppermute | solution.py:143
  20.6 12.1 %collective-permute-start.3 = (bf16[128,1792]{1,0:T(8,128)(2,1)S(1)}, bf16[128,1792]{1,0:T(8,128)(2,1)S(1)}, u32[]{:S(2)}, u32[]{:S(2)}) collective-permute-start(bf16[128,1792]{1,0:T(8,128)(2,1)S(1)} %copy-done.13), channel_id=1, source_target_pairs={{0,2},{1,3},{2,0},{3,1},{4,6},{5,7},{6,4},{7,5},{8,10},{9,11},{10,... | collective-permute-start | bytes 1376264 | tf_op jit(solution)/shard_map/ppermute | solution.py:134
  22.2 12.2 %collective-permute-start.4 = (bf16[128,1792]{1,0:T(8,128)(2,1)S(1)}, bf16[128,1792]{1,0:T(8,128)(2,1)S(1)}, u32[]{:S(2)}, u32[]{:S(2)}) collective-permute-start(bf16[128,1792]{1,0:T(8,128)(2,1)S(1)} %copy-done.13), channel_id=1, source_target_pairs={{0,4},{1,5},{2,6},{3,7},{4,0},{5,1},{6,2},{7,3},{8,12},{9,13},{10,... | collective-permute-start | bytes 1376264 | tf_op jit(solution)/shard_map/ppermute | solution.py:138
  30.9 141.6 %collective-permute-start.19 = (bf16[256,7168]{1,0:T(8,128)(2,1)}, bf16[256,7168]{1,0:T(8,128)(2,1)S(1)}, u32[]{:S(2)}, u32[]{:S(2)}) collective-permute-start(bf16[256,7168]{1,0:T(8,128)(2,1)} %bitcast.119), channel_id=1, source_target_pairs={{0,1},{1,0},{2,3},{3,2},{4,5},{5,4},{6,7},{7,6},{8,9},{9,8},{10,11... | collective-permute-start | bytes 11010056 | tf_op jit(solution)/shard_map/ppermute | solution.py:130
  31.0 146.5 %collective-permute-start.6 = (bf16[7168,512]{1,0:T(8,128)(2,1)}, bf16[7168,512]{1,0:T(8,128)(2,1)}, u32[]{:S(2)}, u32[]{:S(2)}) collective-permute-start(bf16[7168,512]{1,0:T(8,128)(2,1)} %pad_maximum_fusion.1), channel_id=1, source_target_pairs={{0,1},{1,0},{2,3},{3,2},{4,5},{5,4},{6,7},{7,6},{8,9},{9,8},{10,11... | collective-permute-start | bytes 22020104 | tf_op jit(solution)/shard_map/ppermute | solution.py:130
  31.6 15.2 %collective-permute-start.38 = (bf16[128,1792]{1,0:T(8,128)(2,1)S(1)}, bf16[128,1792]{1,0:T(8,128)(2,1)S(1)}, u32[]{:S(2)}, u32[]{:S(2)}) collective-permute-start(bf16[128,1792]{1,0:T(8,128)(2,1)S(1)} %collective-permute-done.34), channel_id=1, source_target_pairs={{0,8},{8,16},{16,24},{24,0},{1,9},{9,17},{17,25},{25,1},{2,10},{10... | collective-permute-start | bytes 1376264 | tf_op jit(solution)/shard_map/ppermute | solution.py:143
  32.7 23.5 %collective-permute-start.35 = (bf16[128,1792]{1,0:T(8,128)(2,1)S(1)}, bf16[128,1792]{1,0:T(8,128)(2,1)S(1)}, u32[]{:S(2)}, u32[]{:S(2)}) collective-permute-start(bf16[128,1792]{1,0:T(8,128)(2,1)S(1)} %collective-permute-done.34), channel_id=1, source_target_pairs={{0,2},{1,3},{2,0},{3,1},{4,6},{5,7},{6,4},{7,5},{8,10},{9,11},{10,... | collective-permute-start | bytes 1376264 | tf_op jit(solution)/shard_map/ppermute | solution.py:134
  34.3 21.4 %collective-permute-start.11 = (bf16[128,1792]{1,0:T(8,128)(2,1)S(1)}, bf16[128,1792]{1,0:T(8,128)(2,1)S(1)}, u32[]{:S(2)}, u32[]{:S(2)}) collective-permute-start(bf16[128,1792]{1,0:T(8,128)(2,1)S(1)} %collective-permute-done.7), channel_id=1, source_target_pairs={{0,8},{8,16},{16,24},{24,0},{1,9},{9,17},{17,25},{25,1},{2,10},{10... | collective-permute-start | bytes 1376264 | tf_op jit(solution)/shard_map/ppermute | solution.py:143
  46.8 11.1 %collective-permute-start.36 = (bf16[128,1792]{1,0:T(8,128)(2,1)S(1)}, bf16[128,1792]{1,0:T(8,128)(2,1)S(1)}, u32[]{:S(2)}, u32[]{:S(2)}) collective-permute-start(bf16[128,1792]{1,0:T(8,128)(2,1)S(1)} %collective-permute-done.34), channel_id=1, source_target_pairs={{0,4},{1,5},{2,6},{3,7},{4,0},{5,1},{6,2},{7,3},{8,12},{9,13},{10,... | collective-permute-start | bytes 1376264 | tf_op jit(solution)/shard_map/ppermute | solution.py:138
  55.7 13.5 %collective-permute-start.33 = (bf16[128,1792]{1,0:T(8,128)(2,1)S(1)}, bf16[128,1792]{1,0:T(8,128)(2,1)S(1)}, u32[]{:S(2)}, u32[]{:S(2)}) collective-permute-start(bf16[128,1792]{1,0:T(8,128)(2,1)S(1)} %collective-permute-done.31), channel_id=1, source_target_pairs={{0,4},{1,5},{2,6},{3,7},{4,0},{5,1},{6,2},{7,3},{8,12},{9,13},{10,... | collective-permute-start | bytes 1376264 | tf_op jit(solution)/shard_map/ppermute | solution.py:138
  56.3 22.7 %collective-permute-start.5 = (bf16[128,1792]{1,0:T(8,128)(2,1)S(1)}, bf16[128,1792]{1,0:T(8,128)(2,1)S(1)}, u32[]{:S(2)}, u32[]{:S(2)}) collective-permute-start(bf16[128,1792]{1,0:T(8,128)(2,1)S(1)} %collective-permute-done.3), channel_id=1, source_target_pairs={{0,4},{1,5},{2,6},{3,7},{4,0},{5,1},{6,2},{7,3},{8,12},{9,13},{10,... | collective-permute-start | bytes 1376264 | tf_op jit(solution)/shard_map/ppermute | solution.py:138
  57.9 21.2 %collective-permute-start.8 = (bf16[128,1792]{1,0:T(8,128)(2,1)S(1)}, bf16[128,1792]{1,0:T(8,128)(2,1)S(1)}, u32[]{:S(2)}, u32[]{:S(2)}) collective-permute-start(bf16[128,1792]{1,0:T(8,128)(2,1)S(1)} %collective-permute-done.7), channel_id=1, source_target_pairs={{0,2},{1,3},{2,0},{3,1},{4,6},{5,7},{6,4},{7,5},{8,10},{9,11},{10,... | collective-permute-start | bytes 1376264 | tf_op jit(solution)/shard_map/ppermute | solution.py:134
  69.2 17.8 %collective-permute-start.9 = (bf16[128,1792]{1,0:T(8,128)(2,1)S(1)}, bf16[128,1792]{1,0:T(8,128)(2,1)S(1)}, u32[]{:S(2)}, u32[]{:S(2)}) collective-permute-start(bf16[128,1792]{1,0:T(8,128)(2,1)S(1)} %collective-permute-done.7), channel_id=1, source_target_pairs={{0,4},{1,5},{2,6},{3,7},{4,0},{5,1},{6,2},{7,3},{8,12},{9,13},{10,... | collective-permute-start | bytes 1376264 | tf_op jit(solution)/shard_map/ppermute | solution.py:138
  79.0 10.6 %collective-permute-start.42 = (bf16[128,1792]{1,0:T(8,128)(2,1)S(1)}, bf16[128,1792]{1,0:T(8,128)(2,1)S(1)}, u32[]{:S(2)}, u32[]{:S(2)}) collective-permute-start(bf16[128,1792]{1,0:T(8,128)(2,1)S(1)} %collective-permute-done.38), channel_id=1, source_target_pairs={{0,8},{8,16},{16,24},{24,0},{1,9},{9,17},{17,25},{25,1},{2,10},{10... | collective-permute-start | bytes 1376264 | tf_op jit(solution)/shard_map/ppermute | solution.py:143
  79.1 21.9 %collective-permute-start.39 = (bf16[128,1792]{1,0:T(8,128)(2,1)S(1)}, bf16[128,1792]{1,0:T(8,128)(2,1)S(1)}, u32[]{:S(2)}, u32[]{:S(2)}) collective-permute-start(bf16[128,1792]{1,0:T(8,128)(2,1)S(1)} %collective-permute-done.38), channel_id=1, source_target_pairs={{0,2},{1,3},{2,0},{3,1},{4,6},{5,7},{6,4},{7,5},{8,10},{9,11},{10,... | collective-permute-start | bytes 1376264 | tf_op jit(solution)/shard_map/ppermute | solution.py:134
  87.0 12.5 %collective-permute-start.15 = (bf16[128,1792]{1,0:T(8,128)(2,1)S(1)}, bf16[128,1792]{1,0:T(8,128)(2,1)S(1)}, u32[]{:S(2)}, u32[]{:S(2)}) collective-permute-start(bf16[128,1792]{1,0:T(8,128)(2,1)S(1)} %collective-permute-done.11), channel_id=1, source_target_pairs={{0,8},{8,16},{16,24},{24,0},{1,9},{9,17},{17,25},{25,1},{2,10},{10... | collective-permute-start | bytes 1376264 | tf_op jit(solution)/shard_map/ppermute | solution.py:143
  89.6 12.0 %collective-permute-start.40 = (bf16[128,1792]{1,0:T(8,128)(2,1)S(1)}, bf16[128,1792]{1,0:T(8,128)(2,1)S(1)}, u32[]{:S(2)}, u32[]{:S(2)}) collective-permute-start(bf16[128,1792]{1,0:T(8,128)(2,1)S(1)} %collective-permute-done.38), channel_id=1, source_target_pairs={{0,4},{1,5},{2,6},{3,7},{4,0},{5,1},{6,2},{7,3},{8,12},{9,13},{10,... | collective-permute-start | bytes 1376264 | tf_op jit(solution)/shard_map/ppermute | solution.py:138
  99.5 13.5 %collective-permute-start.37 = (bf16[128,1792]{1,0:T(8,128)(2,1)S(1)}, bf16[128,1792]{1,0:T(8,128)(2,1)S(1)}, u32[]{:S(2)}, u32[]{:S(2)}) collective-permute-start(bf16[128,1792]{1,0:T(8,128)(2,1)S(1)} %collective-permute-done.36), channel_id=1, source_target_pairs={{0,2},{1,3},{2,0},{3,1},{4,6},{5,7},{6,4},{7,5},{8,10},{9,11},{10,... | collective-permute-start | bytes 1376264 | tf_op jit(solution)/shard_map/ppermute | solution.py:134
  101.0 21.8 %collective-permute-start.12 = (bf16[128,1792]{1,0:T(8,128)(2,1)S(1)}, bf16[128,1792]{1,0:T(8,128)(2,1)S(1)}, u32[]{:S(2)}, u32[]{:S(2)}) collective-permute-start(bf16[128,1792]{1,0:T(8,128)(2,1)S(1)} %collective-permute-done.11), channel_id=1, source_target_pairs={{0,2},{1,3},{2,0},{3,1},{4,6},{5,7},{6,4},{7,5},{8,10},{9,11},{10,... | collective-permute-start | bytes 1376264 | tf_op jit(solution)/shard_map/ppermute | solution.py:134
  101.6 22.6 %collective-permute-start.13 = (bf16[128,1792]{1,0:T(8,128)(2,1)S(1)}, bf16[128,1792]{1,0:T(8,128)(2,1)S(1)}, u32[]{:S(2)}, u32[]{:S(2)}) collective-permute-start(bf16[128,1792]{1,0:T(8,128)(2,1)S(1)} %collective-permute-done.11), channel_id=1, source_target_pairs={{0,4},{1,5},{2,6},{3,7},{4,0},{5,1},{6,2},{7,3},{8,12},{9,13},{10,... | collective-permute-start | bytes 1376264 | tf_op jit(solution)/shard_map/ppermute | solution.py:138
  112.9 19.7 %collective-permute-start.10 = (bf16[128,1792]{1,0:T(8,128)(2,1)S(1)}, bf16[128,1792]{1,0:T(8,128)(2,1)S(1)}, u32[]{:S(2)}, u32[]{:S(2)}) collective-permute-start(bf16[128,1792]{1,0:T(8,128)(2,1)S(1)} %collective-permute-done.9), channel_id=1, source_target_pairs={{0,2},{1,3},{2,0},{3,1},{4,6},{5,7},{6,4},{7,5},{8,10},{9,11},{10,... | collective-permute-start | bytes 1376264 | tf_op jit(solution)/shard_map/ppermute | solution.py:134
  122.7 16.9 %collective-permute-start.43 = (bf16[128,1792]{1,0:T(8,128)(2,1)S(1)}, bf16[128,1792]{1,0:T(8,128)(2,1)S(1)}, u32[]{:S(2)}, u32[]{:S(2)}) collective-permute-start(bf16[128,1792]{1,0:T(8,128)(2,1)S(1)} %collective-permute-done.42), channel_id=1, source_target_pairs={{0,2},{1,3},{2,0},{3,1},{4,6},{5,7},{6,4},{7,5},{8,10},{9,11},{10,... | collective-permute-start | bytes 1376264 | tf_op jit(solution)/shard_map/ppermute | solution.py:134
  124.3 16.9 %collective-permute-start.44 = (bf16[128,1792]{1,0:T(8,128)(2,1)S(1)}, bf16[128,1792]{1,0:T(8,128)(2,1)S(1)}, u32[]{:S(2)}, u32[]{:S(2)}) collective-permute-start(bf16[128,1792]{1,0:T(8,128)(2,1)S(1)} %collective-permute-done.42), channel_id=1, source_target_pairs={{0,4},{1,5},{2,6},{3,7},{4,0},{5,1},{6,2},{7,3},{8,12},{9,13},{10,... | collective-permute-start | bytes 1376264 | tf_op jit(solution)/shard_map/ppermute | solution.py:138
  132.6 24.0 %collective-permute-start.41 = (bf16[128,1792]{1,0:T(8,128)(2,1)S(1)}, bf16[128,1792]{1,0:T(8,128)(2,1)S(1)}, u32[]{:S(2)}, u32[]{:S(2)}) collective-permute-start(bf16[128,1792]{1,0:T(8,128)(2,1)S(1)} %collective-permute-done.39), channel_id=1, source_target_pairs={{0,4},{1,5},{2,6},{3,7},{4,0},{5,1},{6,2},{7,3},{8,12},{9,13},{10,... | collective-permute-start | bytes 1376264 | tf_op jit(solution)/shard_map/ppermute | solution.py:138
  141.2 14.8 %collective-permute-start.17 = (bf16[128,1792]{1,0:T(8,128)(2,1)S(1)}, bf16[128,1792]{1,0:T(8,128)(2,1)S(1)}, u32[]{:S(2)}, u32[]{:S(2)}) collective-permute-start(bf16[128,1792]{1,0:T(8,128)(2,1)S(1)} %collective-permute-done.15), channel_id=1, source_target_pairs={{0,4},{1,5},{2,6},{3,7},{4,0},{5,1},{6,2},{7,3},{8,12},{9,13},{10,... | collective-permute-start | bytes 1376264 | tf_op jit(solution)/shard_map/ppermute | solution.py:138
  148.5 13.7 %collective-permute-start.14 = (bf16[128,1792]{1,0:T(8,128)(2,1)S(1)}, bf16[128,1792]{1,0:T(8,128)(2,1)S(1)}, u32[]{:S(2)}, u32[]{:S(2)}) collective-permute-start(bf16[128,1792]{1,0:T(8,128)(2,1)S(1)} %collective-permute-done.12), channel_id=1, source_target_pairs={{0,4},{1,5},{2,6},{3,7},{4,0},{5,1},{6,2},{7,3},{8,12},{9,13},{10,... | collective-permute-start | bytes 1376264 | tf_op jit(solution)/shard_map/ppermute | solution.py:138
  156.0 10.4 %collective-permute-start.45 = (bf16[128,1792]{1,0:T(8,128)(2,1)S(1)}, bf16[128,1792]{1,0:T(8,128)(2,1)S(1)}, u32[]{:S(2)}, u32[]{:S(2)}) collective-permute-start(bf16[128,1792]{1,0:T(8,128)(2,1)S(1)} %collective-permute-done.44), channel_id=1, source_target_pairs={{0,2},{1,3},{2,0},{3,1},{4,6},{5,7},{6,4},{7,5},{8,10},{9,11},{10,... | collective-permute-start | bytes 1376264 | tf_op jit(solution)/shard_map/ppermute | solution.py:134
  156.6 14.7 %collective-permute-start.18 = (bf16[128,1792]{1,0:T(8,128)(2,1)S(1)}, bf16[128,1792]{1,0:T(8,128)(2,1)S(1)}, u32[]{:S(2)}, u32[]{:S(2)}) collective-permute-start(bf16[128,1792]{1,0:T(8,128)(2,1)S(1)} %collective-permute-done.17), channel_id=1, source_target_pairs={{0,2},{1,3},{2,0},{3,1},{4,6},{5,7},{6,4},{7,5},{8,10},{9,11},{10,... | collective-permute-start | bytes 1376264 | tf_op jit(solution)/shard_map/ppermute | solution.py:134
  237.7 59.4 %collective-permute-start.20 = (bf16[256,1792]{1,0:T(8,128)(2,1)S(1)}, bf16[256,1792]{1,0:T(8,128)(2,1)S(1)}, u32[]{:S(2)}, u32[]{:S(2)}) collective-permute-start(bf16[256,1792]{1,0:T(8,128)(2,1)S(1)} %convolution_convert_fusion.11), channel_id=1, source_target_pairs={{0,4},{1,5},{2,6},{3,7},{4,0},{5,1},{6,2},{7,3},{8,12},{9,13},{10,... | collective-permute-start | bytes 2752520 | tf_op jit(solution)/shard_map/ppermute | solution.py:138
  238.8 99.8 %collective-permute-start.22 = (bf16[256,1792]{1,0:T(8,128)(2,1)S(1)}, bf16[256,1792]{1,0:T(8,128)(2,1)}, u32[]{:S(2)}, u32[]{:S(2)}) collective-permute-start(bf16[256,1792]{1,0:T(8,128)(2,1)S(1)} %convolution_convert_fusion.10), channel_id=1, source_target_pairs={{0,2},{1,3},{2,0},{3,1},{4,6},{5,7},{6,4},{7,5},{8,10},{9,11},{10,... | collective-permute-start | bytes 2752520 | tf_op jit(solution)/shard_map/ppermute | solution.py:134
  247.6 48.2 %collective-permute-start.26 = (bf16[256,1792]{1,0:T(8,128)(2,1)S(1)}, bf16[256,1792]{1,0:T(8,128)(2,1)S(1)}, u32[]{:S(2)}, u32[]{:S(2)}) collective-permute-start(bf16[256,1792]{1,0:T(8,128)(2,1)S(1)} %convolution_convert_fusion.8), channel_id=1, source_target_pairs={{0,2},{1,3},{2,0},{3,1},{4,6},{5,7},{6,4},{7,5},{8,10},{9,11},{10,... | collective-permute-start | bytes 2752520 | tf_op jit(solution)/shard_map/ppermute | solution.py:134
  257.9 14.8 %collective-permute-start.62 = (f32[128,2]{0,1:T(2,128)S(1)}, f32[128,2]{0,1:T(2,128)S(1)}, u32[]{:S(2)}, u32[]{:S(2)}) collective-permute-start(f32[128,2]{0,1:T(2,128)S(1)} %get-tuple-element.44), channel_id=1, source_target_pairs={{0,2},{1,3},{2,0},{3,1},{4,6},{5,7},{6,4},{7,5},{8,10},{9,11},{10,... | collective-permute-start | bytes 3080 | tf_op jit(solution)/shard_map/ppermute | solution.py:134
  263.0 11.3 %collective-permute-start.60 = (f32[128,2]{0,1:T(2,128)S(1)}, f32[128,2]{0,1:T(2,128)S(1)}, u32[]{:S(2)}, u32[]{:S(2)}) collective-permute-start(f32[128,2]{0,1:T(2,128)S(1)} %get-tuple-element.43), channel_id=1, source_target_pairs={{0,2},{1,3},{2,0},{3,1},{4,6},{5,7},{6,4},{7,5},{8,10},{9,11},{10,... | collective-permute-start | bytes 3080 | tf_op jit(solution)/shard_map/ppermute | solution.py:134
  272.7 63.5 %collective-permute-start.24 = (bf16[256,1792]{1,0:T(8,128)(2,1)}, bf16[256,1792]{1,0:T(8,128)(2,1)}, u32[]{:S(2)}, u32[]{:S(2)}) collective-permute-start(bf16[256,1792]{1,0:T(8,128)(2,1)} %convolution_convert_fusion.9), channel_id=1, source_target_pairs={{0,4},{1,5},{2,6},{3,7},{4,0},{5,1},{6,2},{7,3},{8,12},{9,13},{10,... | collective-permute-start | bytes 2752520 | tf_op jit(solution)/shard_map/ppermute | solution.py:138
  274.2 19.5 %collective-permute-start.63 = (f32[128,2]{0,1:T(2,128)S(1)}, f32[128,2]{0,1:T(2,128)S(1)}, u32[]{:S(2)}, u32[]{:S(2)}) collective-permute-start(f32[128,2]{0,1:T(2,128)S(1)} %collective-permute-done.62), channel_id=1, source_target_pairs={{0,4},{1,5},{2,6},{3,7},{4,0},{5,1},{6,2},{7,3},{8,12},{9,13},{10,... | collective-permute-start | bytes 3080 | tf_op jit(solution)/shard_map/ppermute | solution.py:138
  293.7 22.1 %collective-permute-start.46 = (bf16[256,1792]{1,0:T(8,128)(2,1)}, bf16[256,1792]{1,0:T(8,128)(2,1)S(1)}, u32[]{:S(2)}, u32[]{:S(2)}) collective-permute-start(bf16[256,1792]{1,0:T(8,128)(2,1)} %fusion.36), channel_id=1, source_target_pairs={{0,4},{1,5},{2,6},{3,7},{4,0},{5,1},{6,2},{7,3},{8,12},{9,13},{10,... | collective-permute-start | bytes 2752520 | tf_op jit(solution)/shard_map/ppermute | solution.py:138
  295.8 29.8 %collective-permute-start.50 = (bf16[256,1792]{1,0:T(8,128)(2,1)}, bf16[256,1792]{1,0:T(8,128)(2,1)S(1)}, u32[]{:S(2)}, u32[]{:S(2)}) collective-permute-start(bf16[256,1792]{1,0:T(8,128)(2,1)} %fusion.42), channel_id=1, source_target_pairs={{0,4},{1,5},{2,6},{3,7},{4,0},{5,1},{6,2},{7,3},{8,12},{9,13},{10,... | collective-permute-start | bytes 2752520 | tf_op jit(solution)/shard_map/ppermute | solution.py:138
  297.0 31.0 %collective-permute-start.68 = (bf16[256,1792]{1,0:T(8,128)(2,1)}, bf16[256,1792]{1,0:T(8,128)(2,1)}, u32[]{:S(2)}, u32[]{:S(2)}) collective-permute-start(bf16[256,1792]{1,0:T(8,128)(2,1)} %convolution_convert_fusion.7), channel_id=1, source_target_pairs={{0,1},{1,0},{2,3},{3,2},{4,5},{5,4},{6,7},{7,6},{8,9},{9,8},{10,11... | collective-permute-start | bytes 2752520 | tf_op jit(solution)/shard_map/ppermute | solution.py:130
  316.7 14.1 %collective-permute-start.69 = (bf16[256,1792]{1,0:T(8,128)(2,1)}, bf16[256,1792]{1,0:T(8,128)(2,1)}, u32[]{:S(2)}, u32[]{:S(2)}) collective-permute-start(bf16[256,1792]{1,0:T(8,128)(2,1)} %convolution_convert_fusion.6), channel_id=1, source_target_pairs={{0,1},{1,0},{2,3},{3,2},{4,5},{5,4},{6,7},{7,6},{8,9},{9,8},{10,11... | collective-permute-start | bytes 2752520 | tf_op jit(solution)/shard_map/ppermute | solution.py:130
  328.0 23.5 %collective-permute-start.48 = (bf16[256,1792]{1,0:T(8,128)(2,1)}, bf16[256,1792]{1,0:T(8,128)(2,1)}, u32[]{:S(2)}, u32[]{:S(2)}) collective-permute-start(bf16[256,1792]{1,0:T(8,128)(2,1)} %fusion.39), channel_id=1, source_target_pairs={{0,2},{1,3},{2,0},{3,1},{4,6},{5,7},{6,4},{7,5},{8,10},{9,11},{10,... | collective-permute-start | bytes 2752520 | tf_op jit(solution)/shard_map/ppermute | solution.py:134
  330.8 40.0 %collective-permute-start.52 = (bf16[256,1792]{1,0:T(8,128)(2,1)}, bf16[256,1792]{1,0:T(8,128)(2,1)}, u32[]{:S(2)}, u32[]{:S(2)}) collective-permute-start(bf16[256,1792]{1,0:T(8,128)(2,1)} %fusion.45), channel_id=1, source_target_pairs={{0,2},{1,3},{2,0},{3,1},{4,6},{5,7},{6,4},{7,5},{8,10},{9,11},{10,... | collective-permute-start | bytes 2752520 | tf_op jit(solution)/shard_map/ppermute | solution.py:134
  334.3 60.5 %collective-permute-start.64 = (bf16[1792,512]{1,0:T(8,128)(2,1)}, bf16[1792,512]{1,0:T(8,128)(2,1)}, u32[]{:S(2)}, u32[]{:S(2)}) collective-permute-start(bf16[1792,512]{1,0:T(8,128)(2,1)} %convolution_convert_fusion.3), channel_id=1, source_target_pairs={{0,1},{1,0},{2,3},{3,2},{4,5},{5,4},{6,7},{7,6},{8,9},{9,8},{10,11... | collective-permute-start | bytes 5505032 | tf_op jit(solution)/shard_map/ppermute | solution.py:130
  336.2 63.1 %collective-permute-start.65 = (bf16[1792,512]{1,0:T(8,128)(2,1)}, bf16[1792,512]{1,0:T(8,128)(2,1)}, u32[]{:S(2)}, u32[]{:S(2)}) collective-permute-start(bf16[1792,512]{1,0:T(8,128)(2,1)} %convolution_convert_fusion.2), channel_id=1, source_target_pairs={{0,1},{1,0},{2,3},{3,2},{4,5},{5,4},{6,7},{7,6},{8,9},{9,8},{10,11... | collective-permute-start | bytes 5505032 | tf_op jit(solution)/shard_map/ppermute | solution.py:130
  338.6 37.8 %collective-permute-start.71 = (bf16[256,1792]{1,0:T(8,128)(2,1)}, bf16[256,1792]{1,0:T(8,128)(2,1)S(1)}, u32[]{:S(2)}, u32[]{:S(2)}) collective-permute-start(bf16[256,1792]{1,0:T(8,128)(2,1)} %convolution_convert_fusion.4), channel_id=1, source_target_pairs={{0,1},{1,0},{2,3},{3,2},{4,5},{5,4},{6,7},{7,6},{8,9},{9,8},{10,11... | collective-permute-start | bytes 2752520 | tf_op jit(solution)/shard_map/ppermute | solution.py:130
  351.5 52.5 %collective-permute-start.66 = (bf16[1792,512]{1,0:T(8,128)(2,1)}, bf16[1792,512]{1,0:T(8,128)(2,1)}, u32[]{:S(2)}, u32[]{:S(2)}) collective-permute-start(bf16[1792,512]{1,0:T(8,128)(2,1)} %convolution_convert_fusion.1), channel_id=1, source_target_pairs={{0,1},{1,0},{2,3},{3,2},{4,5},{5,4},{6,7},{7,6},{8,9},{9,8},{10,11... | collective-permute-start | bytes 5505032 | tf_op jit(solution)/shard_map/ppermute | solution.py:130
  370.8 12.2 %collective-permute-start.27 = (bf16[128,1792]{1,0:T(8,128)(2,1)S(1)}, bf16[128,1792]{1,0:T(8,128)(2,1)S(1)}, u32[]{:S(2)}, u32[]{:S(2)}) collective-permute-start(bf16[128,1792]{1,0:T(8,128)(2,1)S(1)} %slice.445), channel_id=1, source_target_pairs={{0,4},{1,5},{2,6},{3,7},{4,0},{5,1},{6,2},{7,3},{8,12},{9,13},{10,... | collective-permute-start | bytes 1376264 | tf_op jit(solution)/shard_map/ppermute | solution.py:138
  376.8 32.0 %collective-permute-start.67 = (bf16[1792,512]{1,0:T(8,128)(2,1)S(1)}, bf16[1792,512]{1,0:T(8,128)(2,1)S(1)}, u32[]{:S(2)}, u32[]{:S(2)}) collective-permute-start(bf16[1792,512]{1,0:T(8,128)(2,1)S(1)} %copy-done.32), channel_id=1, source_target_pairs={{0,1},{1,0},{2,3},{3,2},{4,5},{5,4},{6,7},{7,6},{8,9},{9,8},{10,11... | collective-permute-start | bytes 5505032 | tf_op jit(solution)/shard_map/ppermute | solution.py:130
  382.9 11.3 %collective-permute-start.53 = (bf16[128,1792]{1,0:T(8,128)(2,1)S(1)}, bf16[128,1792]{1,0:T(8,128)(2,1)S(1)}, u32[]{:S(2)}, u32[]{:S(2)}) collective-permute-start(bf16[128,1792]{1,0:T(8,128)(2,1)S(1)} %slice.441), channel_id=1, source_target_pairs={{0,4},{1,5},{2,6},{3,7},{4,0},{5,1},{6,2},{7,3},{8,12},{9,13},{10,... | collective-permute-start | bytes 1376264 | tf_op jit(solution)/shard_map/ppermute | solution.py:138
  394.2 17.3 %collective-permute-start.25 = (bf16[128,1792]{1,0:T(8,128)(2,1)S(1)}, bf16[128,1792]{1,0:T(8,128)(2,1)S(1)}, u32[]{:S(2)}, u32[]{:S(2)}) collective-permute-start(bf16[128,1792]{1,0:T(8,128)(2,1)S(1)} %slice.446), channel_id=1, source_target_pairs={{0,2},{1,3},{2,0},{3,1},{4,6},{5,7},{6,4},{7,5},{8,10},{9,11},{10,... | collective-permute-start | bytes 1376264 | tf_op jit(solution)/shard_map/ppermute | solution.py:134
  394.8 36.3 %collective-permute-start.23 = (bf16[128,1792]{1,0:T(8,128)(2,1)S(1)}, bf16[128,1792]{1,0:T(8,128)(2,1)S(1)}, u32[]{:S(2)}, u32[]{:S(2)}) collective-permute-start(bf16[128,1792]{1,0:T(8,128)(2,1)S(1)} %slice.447), channel_id=1, source_target_pairs={{0,4},{1,5},{2,6},{3,7},{4,0},{5,1},{6,2},{7,3},{8,12},{9,13},{10,... | collective-permute-start | bytes 1376264 | tf_op jit(solution)/shard_map/ppermute | solution.py:138
  399.4 56.8 %collective-permute-start.21 = (bf16[128,1792]{1,0:T(8,128)(2,1)S(1)}, bf16[128,1792]{1,0:T(8,128)(2,1)S(1)}, u32[]{:S(2)}, u32[]{:S(2)}) collective-permute-start(bf16[128,1792]{1,0:T(8,128)(2,1)S(1)} %slice.448), channel_id=1, source_target_pairs={{0,2},{1,3},{2,0},{3,1},{4,6},{5,7},{6,4},{7,5},{8,10},{9,11},{10,... | collective-permute-start | bytes 1376264 | tf_op jit(solution)/shard_map/ppermute | solution.py:134
  404.0 20.6 %collective-permute-start.51 = (bf16[128,1792]{1,0:T(8,128)(2,1)S(1)}, bf16[128,1792]{1,0:T(8,128)(2,1)S(1)}, u32[]{:S(2)}, u32[]{:S(2)}) collective-permute-start(bf16[128,1792]{1,0:T(8,128)(2,1)S(1)} %slice.442), channel_id=1, source_target_pairs={{0,2},{1,3},{2,0},{3,1},{4,6},{5,7},{6,4},{7,5},{8,10},{9,11},{10,... | collective-permute-start | bytes 1376264 | tf_op jit(solution)/shard_map/ppermute | solution.py:134
  408.9 11.3 %collective-permute-start.28 = (bf16[128,1792]{1,0:T(8,128)(2,1)S(1)}, bf16[128,1792]{1,0:T(8,128)(2,1)S(1)}, u32[]{:S(2)}, u32[]{:S(2)}) collective-permute-start(bf16[128,1792]{1,0:T(8,128)(2,1)S(1)} %fusion.90), channel_id=1, source_target_pairs={{0,8},{8,16},{16,24},{24,0},{1,9},{9,17},{17,25},{25,1},{2,10},{10... | collective-permute-start | bytes 1376264 | tf_op jit(solution)/shard_map/ppermute | solution.py:143
  411.5 34.9 %collective-permute-start.49 = (bf16[128,1792]{1,0:T(8,128)(2,1)S(1)}, bf16[128,1792]{1,0:T(8,128)(2,1)S(1)}, u32[]{:S(2)}, u32[]{:S(2)}) collective-permute-start(bf16[128,1792]{1,0:T(8,128)(2,1)S(1)} %slice.443), channel_id=1, source_target_pairs={{0,4},{1,5},{2,6},{3,7},{4,0},{5,1},{6,2},{7,3},{8,12},{9,13},{10,... | collective-permute-start | bytes 1376264 | tf_op jit(solution)/shard_map/ppermute | solution.py:138
  420.2 10.7 %collective-permute-start.54 = (bf16[128,1792]{1,0:T(8,128)(2,1)S(1)}, bf16[128,1792]{1,0:T(8,128)(2,1)S(1)}, u32[]{:S(2)}, u32[]{:S(2)}) collective-permute-start(bf16[128,1792]{1,0:T(8,128)(2,1)S(1)} %fusion.83), channel_id=1, source_target_pairs={{0,8},{8,16},{16,24},{24,0},{1,9},{9,17},{17,25},{25,1},{2,10},{10... | collective-permute-start | bytes 1376264 | tf_op jit(solution)/shard_map/ppermute | solution.py:143
  424.5 41.4 %collective-permute-start.47 = (bf16[128,1792]{1,0:T(8,128)(2,1)S(1)}, bf16[128,1792]{1,0:T(8,128)(2,1)S(1)}, u32[]{:S(2)}, u32[]{:S(2)}) collective-permute-start(bf16[128,1792]{1,0:T(8,128)(2,1)S(1)} %slice.444), channel_id=1, source_target_pairs={{0,2},{1,3},{2,0},{3,1},{4,6},{5,7},{6,4},{7,5},{8,10},{9,11},{10,... | collective-permute-start | bytes 1376264 | tf_op jit(solution)/shard_map/ppermute | solution.py:134
  430.9 15.3 %collective-permute-start.29 = (bf16[128,1792]{1,0:T(8,128)(2,1)S(1)}, bf16[128,1792]{1,0:T(8,128)(2,1)S(1)}, u32[]{:S(2)}, u32[]{:S(2)}) collective-permute-start(bf16[128,1792]{1,0:T(8,128)(2,1)S(1)} %fusion.92), channel_id=1, source_target_pairs={{0,8},{8,16},{16,24},{24,0},{1,9},{9,17},{17,25},{25,1},{2,10},{10... | collective-permute-start | bytes 1376264 | tf_op jit(solution)/shard_map/ppermute | solution.py:143
  431.1 24.9 %collective-permute-start.55 = (bf16[128,1792]{1,0:T(8,128)(2,1)S(1)}, bf16[128,1792]{1,0:T(8,128)(2,1)S(1)}, u32[]{:S(2)}, u32[]{:S(2)}) collective-permute-start(bf16[128,1792]{1,0:T(8,128)(2,1)S(1)} %fusion.85), channel_id=1, source_target_pairs={{0,8},{8,16},{16,24},{24,0},{1,9},{9,17},{17,25},{25,1},{2,10},{10... | collective-permute-start | bytes 1376264 | tf_op jit(solution)/shard_map/ppermute | solution.py:143
  446.3 18.7 %collective-permute-start.30 = (bf16[128,1792]{1,0:T(8,128)(2,1)S(1)}, bf16[128,1792]{1,0:T(8,128)(2,1)S(1)}, u32[]{:S(2)}, u32[]{:S(2)}) collective-permute-start(bf16[128,1792]{1,0:T(8,128)(2,1)S(1)} %fusion.94), channel_id=1, source_target_pairs={{0,8},{8,16},{16,24},{24,0},{1,9},{9,17},{17,25},{25,1},{2,10},{10... | collective-permute-start | bytes 1376264 | tf_op jit(solution)/shard_map/ppermute | solution.py:143
  456.1 13.8 %collective-permute-start.56 = (bf16[128,1792]{1,0:T(8,128)(2,1)S(1)}, bf16[128,1792]{1,0:T(8,128)(2,1)S(1)}, u32[]{:S(2)}, u32[]{:S(2)}) collective-permute-start(bf16[128,1792]{1,0:T(8,128)(2,1)S(1)} %fusion.87), channel_id=1, source_target_pairs={{0,8},{8,16},{16,24},{24,0},{1,9},{9,17},{17,25},{25,1},{2,10},{10... | collective-permute-start | bytes 1376264 | tf_op jit(solution)/shard_map/ppermute | solution.py:143
  (42 other events, 842.8 us)
